TPU v7x, 1024 devices: a whole 4x4x32 slice. The times are simulated.
1024 devices in a mesh: fsdp: 32 (over z), dp: 4 (over y), mp: 8 (over x, core).
Axes of the slice: x: 4, y: 4, z: 32, core: 2. Of those that a mesh axis runs over, the one named last changes fastest.
Arguments:
- grad_parts: bfloat16 [4, 1024, 256, 256], P('dp', 'mp', 'fsdp'), may hold values from -6 to 6
- owner_ids: int32 [1024, 1], P('mp'), may hold values from 0 to 31; in each aligned block of 32 rows (0 to 31, 32 to 63, ...) at most 2 rows name the same one
- factors: float32 [8, 4, 64, 2, 256, 256], P('mp', 'dp', 'fsdp'), as said below
Outputs:
- directions: bfloat16 [1024, 256, 256], P('mp', 'fsdp')
- new_factors: float32 [8, 4, 64, 2, 256, 256], P('mp', 'dp', 'fsdp')
Inputs may be any that keep to these rules, and one draw needn't show every extreme that they name: `owner_ids`: in each aligned block of 32 rows (the blocks of one group) no owner is named more than 2 times, a bound that some block reaches. `factors`: every factor is symmetric and each diagonal entry exceeds the sum of magnitudes of the other entries of its row.
All inputs are finite; a program needn't handle non-finite values. Where the computation divides by a largest or mean magnitude, that divisor is 1e-20 or more.
Results may differ from a plain program's by a relative error of at most 0.015.
Values may be sent and summed in bfloat16 or wider, within the bound.
No kernel may reach another device: no remote copies, remote signals or barrier semaphores. Data moves between devices by JAX's collectives and lax.ppermute only.
A program may use at most 32 MiB of HBM per device.

v0:
```python
import jax
import jax.numpy as jnp
from jax import lax
from jax.sharding import PartitionSpec as P

decay_rate = 0.95
epsilon = 1e-06


def slot_ranks(owners):
    positions = jnp.arange(owners.shape[0])
    same_owner = owners[:, None] == owners[None, :]
    earlier = positions[None, :] < positions[:, None]
    return jnp.sum(jnp.where(same_owner & earlier, 1, 0), axis=1).astype(jnp.int32)


def batched_product(first_term, second_term):
    return jnp.einsum("sij,sjk->sik", first_term, second_term, precision=lax.Precision.HIGHEST)


def inverse_root(factor):
    row_bound = jnp.max(jnp.sum(jnp.abs(factor), axis=2), axis=1) + epsilon
    normed = factor / row_bound[:, None, None]
    identity = jnp.eye(factor.shape[1], dtype=jnp.float32)
    first_step = (5.0 * identity - normed) * 0.25
    squared = batched_product(first_step, first_step)
    fourth_power = batched_product(squared, squared)
    shifted = batched_product(fourth_power, normed)
    second_step = (5.0 * identity - shifted) * 0.25
    return batched_product(first_step, second_step)


def precondition(blocks, left_prev, right_prev, used_slots):
    left_factor = decay_rate * left_prev + jnp.einsum(
        "sij,skj->sik", blocks, blocks, preferred_element_type=jnp.float32
    )
    right_factor = decay_rate * right_prev + jnp.einsum(
        "sji,sjk->sik", blocks, blocks, preferred_element_type=jnp.float32
    )
    left_root = inverse_root(left_factor).astype(jnp.bfloat16)
    right_root = inverse_root(right_factor).astype(jnp.bfloat16)
    half_product = jnp.einsum(
        "sij,sjk->sik", left_root, blocks, preferred_element_type=jnp.float32
    ).astype(jnp.bfloat16)
    raw_direction = jnp.einsum(
        "sij,sjk->sik", half_product, right_root, preferred_element_type=jnp.float32
    )
    widened = blocks.astype(jnp.float32)
    grad_scale = jnp.sqrt(jnp.mean(widened * widened, axis=(1, 2)) + epsilon)
    own_scale = jnp.sqrt(jnp.mean(raw_direction * raw_direction, axis=(1, 2)) + epsilon)
    direction = (raw_direction * (grad_scale / own_scale)[:, None, None]).astype(jnp.bfloat16)
    keep_mask = used_slots[:, None, None]
    return (
        jnp.where(keep_mask, left_factor, left_prev),
        jnp.where(keep_mask, right_factor, right_prev),
        direction,
    )


def body(grad_parts, owner_ids, factors):
    fsdp_count = lax.axis_size("fsdp")
    replica_count = lax.axis_size("dp")
    slot_count = factors.shape[2]
    row_count = grad_parts.shape[2]
    block_width = grad_parts.shape[3]
    group_blocks = grad_parts.shape[1] // replica_count
    my_replica = lax.axis_index("dp")
    my_fsdp = lax.axis_index("fsdp")
    owner_groups = owner_ids[:, 0].reshape(replica_count, group_blocks)
    place_groups = jax.vmap(slot_ranks)(owner_groups) * fsdp_count + owner_groups
    my_owners = lax.dynamic_index_in_dim(owner_groups, my_replica, 0, keepdims=False)
    my_places = lax.dynamic_index_in_dim(place_groups, my_replica, 0, keepdims=False)
    summed = lax.psum_scatter(
        grad_parts.astype(jnp.float32).astype(jnp.bfloat16), "dp", scatter_dimension=1, tiled=True
    ).astype(jnp.float32)
    reduced = summed[0].astype(jnp.bfloat16)
    empty_slots = jnp.zeros((slot_count * fsdp_count, row_count, block_width), jnp.bfloat16)
    outgoing = (
        empty_slots.at[my_places]
        .set(reduced)
        .reshape(slot_count, fsdp_count, row_count, block_width)
    )
    arrived = lax.all_to_all(outgoing, "fsdp", split_axis=1, concat_axis=1, tiled=True)
    blocks = arrived.reshape(slot_count, fsdp_count * row_count, block_width)
    slot_state = factors[0, 0]
    live_count = jnp.sum(jnp.where(my_owners == my_fsdp, 1, 0))
    used_slots = jnp.arange(slot_count) < live_count
    left_new, right_new, direction = precondition(
        blocks, slot_state[:, 0], slot_state[:, 1], used_slots
    )
    new_state = jnp.stack([left_new, right_new], axis=1)[None, None]
    every_group = lax.all_gather(direction[None], "dp", axis=0, tiled=True)
    homeward = every_group.reshape(replica_count, slot_count, fsdp_count, row_count, block_width)
    returned = lax.all_to_all(homeward, "fsdp", split_axis=2, concat_axis=2, tiled=True)
    flat_rows = returned.reshape(replica_count, slot_count * fsdp_count, row_count, block_width)
    picked = jax.vmap(lambda rows_all, places: jnp.take(rows_all, places, axis=0))(
        flat_rows, place_groups
    )
    directions = picked.reshape(replica_count * group_blocks, row_count, block_width)
    return (directions, new_state)


def solution(mesh):
    return jax.shard_map(
        body,
        mesh=mesh,
        in_specs=(
            P("dp", "mp", "fsdp", None),
            P("mp", None),
            P("mp", "dp", "fsdp", None, None, None),
        ),
        out_specs=(P("mp", "fsdp", None), P("mp", "dp", "fsdp", None, None, None)),
        check_vma=False,
    )
```

profile of v0, /device:TPU:6, one launch (start us, length us, event | category | flops | bytes accessed | tf_op | source)
XLA Modules:
  0.0 296.6 jit_solution(15905116519971993029)
XLA Ops:
  7.2 0.0 copy-start
  7.2 0.0 reduce-scatter.2.cloned.1.call-start
  7.2 0.7 reduce-scatter.2.cloned.1.call-update
  7.9 0.5 broadcast.179
  8.4 1.3 reduce.7
  9.7 0.1 eq.38
  9.8 0.2 select_reduce_fusion
  10.1 48.1 %reduce-scatter.2.cloned.1.call-done = bf16[1,32,8,256]{3,2,1,0:T(8,128)(2,1)} async-done(((bf16[1,128,8,256]{3,2,1,0:T(8,128)(2,1)}), bf16[1,32,8,256]{3,2,1,0:T(8,128)(2,1)}) %reduce-scatter.2.cloned.1.call-update) | async-done | bytes 131088 | tf_op jit(solution)/shard_map/reduce_scatter | solution.py:73
  58.2 2.6 scatter_fusion
  60.8 0.7 copy.49
  61.5 22.9 %all-to-all-start = ((bf16[2,32,8,256]{3,2,0,1:T(8,128)(2,1)}), bf16[2,32,8,256]{3,2,0,1:T(8,128)(2,1)S(1)}, u32[]{:S(2)}, u32[]{:S(2)}) async-start(bf16[2,32,8,256]{3,2,0,1:T(8,128)(2,1)} %copy.49), calls=%async_computation.1 | async-start | bytes 524288 | tf_op jit(solution)/shard_map/all_to_all | solution.py:83
  84.5 0.0 all-gather.3.cloned.1.call-start
  84.5 0.0 copy-done
  84.6 0.3 copy.48
  84.9 0.6 fusion.25
  85.5 0.6 iota_compare_fusion.2
  86.2 0.7 fusion.17
  86.9 38.6 %all-to-all-done = bf16[2,32,8,256]{3,2,0,1:T(8,128)(2,1)S(1)} async-done(((bf16[2,32,8,256]{3,2,0,1:T(8,128)(2,1)}), bf16[2,32,8,256]{3,2,0,1:T(8,128)(2,1)S(1)}, u32[]{:S(2)}, u32[]{:S(2)}) %all-to-all-start) | async-done | bytes 262176 | tf_op jit(solution)/shard_map/all_to_all | solution.py:83
  125.5 0.3 convolution_add_fusion
  125.7 0.3 convolution_add_fusion.1
  126.0 0.2 select_bitcast_fusion.1
  126.2 0.1 reduce_max.19
  126.4 0.1 reduce_max.18
  126.5 2.2 fusion.4
  128.7 0.0 copy-start.1
  128.7 0.6 fusion.35
  129.4 0.3 copy-done.1
  129.7 0.7 fusion
  130.4 1.1 convolution_convert_fusion.1
  131.5 1.2 fusion.3
  132.7 0.6 fusion.34
  133.3 0.7 fusion.1
  134.0 1.1 convolution_convert_fusion.2
  135.2 0.2 multiply_reduce_fusion.1
  135.3 0.5 multiply_reduce_fusion
  135.8 0.8 multiply_convert_fusion
  136.6 0.0 all-gather.3.cloned.1.call-update
  136.7 21.7 %all-gather.3.cloned.1.call-done = bf16[8,256,256]{2,1,0:T(8,128)(2,1)} async-done(((bf16[2,256,256]{2,1,0:T(8,128)(2,1)}), bf16[8,256,256]{2,1,0:T(8,128)(2,1)}) %all-gather.3.cloned.1.call-update) | async-done | bytes 1048592 | tf_op jit(solution)/shard_map/all_gather | solution.py:92
  158.3 2.4 copy.64
  160.7 22.9 %all-to-all-start.1 = ((bf16[4,2,32,8,256]{4,3,1,0,2:T(8,128)(2,1)}), bf16[4,2,32,8,256]{4,3,1,0,2:T(8,128)(2,1)S(1)}, u32[]{:S(2)}, u32[]{:S(2)}) async-start(bf16[4,2,32,8,256]{4,3,1,0,2:T(8,128)(2,1)} %copy.64), calls=%async_computation.2 | async-start | bytes 2097152 | tf_op jit(solution)/shard_map/all_to_all | solution.py:94
  183.6 0.0 copy-start.2
  183.6 0.6 copy-done.2
  184.3 0.1 reshape_squeeze.3
  184.4 0.1 reshape.139
  184.5 0.1 mul.69
  184.6 0.1 maximum_bitcast_fusion
  184.6 1.3 copy.66
  186.0 101.8 %all-to-all-done.1 = bf16[4,2,32,8,256]{4,3,1,0,2:T(8,128)(2,1)S(1)} async-done(((bf16[4,2,32,8,256]{4,3,1,0,2:T(8,128)(2,1)}), bf16[4,2,32,8,256]{4,3,1,0,2:T(8,128)(2,1)S(1)}, u32[]{:S(2)}, u32[]{:S(2)}) %all-to-all-start.1) | async-done | bytes 1048608 | tf_op jit(solution)/shard_map/all_to_all | solution.py:94
  287.8 0.1 copy.65
  287.9 0.9 gather_fusion
  288.7 1.0 broadcast_select_fusion
  (9 shorter events, 0.1 us)
Async XLA Ops:
  7.2 77.4 %copy-start = (f32[1,1,2,2,256,256]{5,4,3,2,1,0:T(8,128)S(1)}, f32[1,1,2,2,256,256]{5,4,3,2,1,0:T(8,128)}, u32[]{:S(2)}) copy-start(f32[1,1,2,2,256,256]{5,4,3,2,1,0:T(8,128)} %param.5) | copy-start | bytes 3145732
  7.2 51.0 %reduce-scatter.2.cloned.1.call-start = ((), (), s32[]{:S(2)}) async-start(), calls=%async_computation.3 | async-start | bytes 655360 | tf_op jit(solution)/shard_map/reduce_scatter | solution.py:73
  61.5 63.9 %all-to-all-start = ((bf16[2,32,8,256]{3,2,0,1:T(8,128)(2,1)}), bf16[2,32,8,256]{3,2,0,1:T(8,128)(2,1)S(1)}, u32[]{:S(2)}, u32[]{:S(2)}) async-start(bf16[2,32,8,256]{3,2,0,1:T(8,128)(2,1)} %copy.49), calls=%async_computation.1 | async-start | bytes 524288 | tf_op jit(solution)/shard_map/all_to_all | solution.py:83
  84.5 73.8 %all-gather.3.cloned.1.call-start = ((), (), s32[]{:S(2)}) async-start(), calls=%async_computation.4 | async-start | bytes 1310720 | tf_op jit(solution)/shard_map/all_gather | solution.py:92
  128.7 1.0 copy-start.1
  160.7 127.1 %all-to-all-start.1 = ((bf16[4,2,32,8,256]{4,3,1,0,2:T(8,128)(2,1)}), bf16[4,2,32,8,256]{4,3,1,0,2:T(8,128)(2,1)S(1)}, u32[]{:S(2)}, u32[]{:S(2)}) async-start(bf16[4,2,32,8,256]{4,3,1,0,2:T(8,128)(2,1)} %copy.64), calls=%async_computation.2 | async-start | bytes 2097152 | tf_op jit(solution)/shard_map/all_to_all | solution.py:94
  183.6 0.7 copy-start.2
Sparse Core Ops, SparseCore 0:
  11.4 46.7 reduce-scatter.1
  136.8 21.4 all-gather.2
where the time goes:
time: 298 us; the launch traced here: 297 us
  waiting for transfers between devices  211 us (71%)
  starting transfers between devices  45.9 us (15%)
  between operations  14.2 us (5%)
  local copies, waits for them, and re-layouts  10.1 us (3%)
  matrix products  9.31 us (3%)
  other arithmetic  6.15 us (2%)
    all_to_all x1, waiting for transfers between devices, body(): lax.all_to_all(homeward, 'fsdp', split_axis=2, concat_axis=2, tiled=True)  102 us
    reduce_scatter x1, waiting for transfers between devices, body(): lax.psum_scatter(grad_parts.astype(jnp.float32).astype(jnp.bfloat16), 'dp...  48.1 us
    all_to_all x1, waiting for transfers between devices, body(): lax.all_to_all(outgoing, 'fsdp', split_axis=1, concat_axis=1, tiled=True)  38.6 us
    all_to_all x1, starting transfers between devices, body(): lax.all_to_all(outgoing, 'fsdp', split_axis=1, concat_axis=1, tiled=True)  22.9 us
    all_to_all x1, starting transfers between devices, body(): lax.all_to_all(homeward, 'fsdp', split_axis=2, concat_axis=2, tiled=True)  22.9 us
    all_gather x1, waiting for transfers between devices, body(): every_group = lax.all_gather(direction[None], 'dp', axis=0, tiled=True)  21.7 us
    dot_general x8, matrix products, batched_product(): jnp.einsum('sij,sjk->sik', first_term, second_term, precision=lax.Precisi...  8.32 us
  transfers between devices with their start and end apart: 4, of which 4 were waited for; matrix products, arithmetic and copies ran while one was open for 2% of the time, Pallas kernels for 0%

commit v1 on v0

v1 whole, which is shorter than its diff:
```python
import numpy as np
import jax
import jax.numpy as jnp
from jax import lax
from jax.experimental import pallas as pl
from jax.experimental.pallas import tpu as pltpu
from jax.sharding import PartitionSpec as P

decay_rate = 0.95
epsilon = 1e-06
centre = 0.5


def root_coefficients():
    x = np.polynomial.Polynomial([centre, 1.0])
    t0 = (5.0 - x) / 4.0
    t1 = (5.0 - t0**4 * x) / 4.0
    return [float(c) for c in (t0 * t1).coef]


def dot(a, b, contract):
    return lax.dot_general(a, b, ((contract[:1], contract[1:]), ((), ())), preferred_element_type=jnp.float32)


def inverse_root(factor, eye):
    r = root_coefficients()
    bound = jnp.max(jnp.sum(jnp.abs(factor), axis=0, keepdims=True), axis=1, keepdims=True) + epsilon
    m = factor * (1.0 / bound) - centre * eye
    mh = m.astype(jnp.bfloat16)
    m2 = dot(mh, mh, (1, 0))
    m2h = m2.astype(jnp.bfloat16)
    u = r[4] * eye + r[5] * m + r[6] * m2
    v = r[3] * m + dot(m2h, u.astype(jnp.bfloat16), (1, 0))
    return r[0] * eye + r[1] * m + r[2] * m2 + dot(m2h, v.astype(jnp.bfloat16), (1, 0))


def place_kernel(owners, parts, out, seen):
    out[...] = jnp.zeros_like(out)
    replicas, count = parts.shape[:2]
    first = lax.axis_index("dp") * count

    def clear(i, _):
        seen[i] = 0
        return 0

    lax.fori_loop(0, out.shape[0], clear, 0)

    def step(b, _):
        owner = owners[first + b]
        slot = seen[owner]
        seen[owner] = slot + 1
        total = parts[0, b].astype(jnp.float32)
        for r in range(1, replicas):
            total = total + parts[r, b].astype(jnp.float32)
        out[owner, slot] = total.astype(out.dtype)
        return 0

    lax.fori_loop(0, count, step, 0, unroll=True)


def pick_kernel(owners, rows, out, seen):
    count = out.shape[0]
    first = lax.axis_index("dp") * count

    def clear(i, _):
        seen[i] = 0
        return 0

    lax.fori_loop(0, rows.shape[0], clear, 0)

    def step(b, _):
        owner = owners[first + b]
        slot = seen[owner]
        seen[owner] = slot + 1
        out[b] = rows[owner, slot]
        return 0

    lax.fori_loop(0, count, step, 0, unroll=True)


def precondition_kernel(owners, rows, factors, out, state):
    count = rows.shape[0]
    first = lax.axis_index("dp") * count
    me = lax.axis_index("fsdp")
    order = factors.shape[-1]
    live = lax.fori_loop(0, count, lambda b, n: n + jnp.where(owners[first + b] == me, 1, 0), 0, unroll=True)
    eye = (
        lax.broadcasted_iota(jnp.int32, (order, order), 0) == lax.broadcasted_iota(jnp.int32, (order, order), 1)
    ).astype(jnp.float32)
    for s in range(factors.shape[0]):
        wide = rows[:, s].astype(jnp.float32).reshape(order, order)
        g = wide.astype(jnp.bfloat16)
        left = decay_rate * factors[s, 0] + dot(g, g, (1, 1))
        right = decay_rate * factors[s, 1] + dot(g, g, (0, 0))
        used = s < live
        state[s, 0] = jnp.where(used, left, factors[s, 0])
        state[s, 1] = jnp.where(used, right, factors[s, 1])
        left_root = inverse_root(left, eye).astype(jnp.bfloat16)
        right_root = inverse_root(right, eye).astype(jnp.bfloat16)
        half = dot(left_root, g, (1, 0)).astype(jnp.bfloat16)
        raw = dot(half, right_root, (1, 0))

        def mean_square(x):
            return jnp.sum(jnp.sum(x * x, axis=0, keepdims=True), axis=1, keepdims=True) / (order * order)

        ratio = jnp.sqrt(mean_square(wide) + epsilon) / jnp.sqrt(mean_square(raw) + epsilon)
        out[:, s] = (raw * ratio).reshape(rows.shape[0], rows.shape[2], order).astype(out.dtype)


def body(grad_parts, owner_ids, factors):
    fsdp_count = lax.axis_size("fsdp")
    replica_count = lax.axis_size("dp")
    slot_count = factors.shape[2]
    row_count, width = grad_parts.shape[2:]
    group_blocks = grad_parts.shape[1] // replica_count
    owners = owner_ids.reshape(-1)
    vmem = pl.BlockSpec(memory_space=pltpu.VMEM)
    smem = pl.BlockSpec(memory_space=pltpu.SMEM)
    seen = pltpu.SMEM((fsdp_count,), jnp.int32)
    params = pltpu.CompilerParams(vmem_limit_bytes=32 * 1024 * 1024)
    wire = jax.ShapeDtypeStruct((fsdp_count, slot_count, row_count, width), jnp.bfloat16)

    mine = grad_parts.reshape(replica_count, group_blocks, row_count, width)
    parts = lax.all_to_all(mine, "dp", split_axis=0, concat_axis=0, tiled=True)
    outgoing = pl.pallas_call(
        place_kernel,
        out_shape=wire,
        in_specs=[smem, vmem],
        out_specs=vmem,
        scratch_shapes=[seen],
        compiler_params=params,
        name="sum_and_place",
    )(owners, parts)
    arrived = lax.all_to_all(outgoing, "fsdp", split_axis=0, concat_axis=0, tiled=True)
    directions, state = pl.pallas_call(
        precondition_kernel,
        out_shape=(wire, jax.ShapeDtypeStruct(factors.shape[2:], factors.dtype)),
        in_specs=[smem, vmem, vmem],
        out_specs=(vmem, vmem),
        compiler_params=params,
        name="precondition",
    )(owners, arrived, factors[0, 0])
    returned = lax.all_to_all(directions, "fsdp", split_axis=0, concat_axis=0, tiled=True)
    picked = pl.pallas_call(
        pick_kernel,
        out_shape=jax.ShapeDtypeStruct((group_blocks, row_count, width), jnp.bfloat16),
        in_specs=[smem, vmem],
        out_specs=vmem,
        scratch_shapes=[seen],
        compiler_params=params,
        name="pick",
    )(owners, returned)
    gathered = lax.all_gather(picked, "dp", axis=0, tiled=True)
    return gathered, state[None, None]


def solution(mesh):
    return jax.shard_map(
        body,
        mesh=mesh,
        in_specs=(
            P("dp", "mp", "fsdp", None),
            P("mp", None),
            P("mp", "dp", "fsdp", None, None, None),
        ),
        out_specs=(P("mp", "fsdp", None), P("mp", "dp", "fsdp", None, None, None)),
        check_vma=False,
    )
```

time: 298 us -> 148 us (0.50)
  waiting for transfers between devices: 211 us -> 0 us
  blocking collectives: 0 us -> 141 us
  starting transfers between devices: 45.9 us -> 0 us
  between operations: 14.2 us -> 0.66 us
  matrix products: 9.31 us -> 0 us
  local copies, waits for them, and re-layouts: 10.1 us -> 1.45 us
  other arithmetic: 6.15 us -> 0 us
  Pallas kernels: 0 us -> 4.85 us
    all_to_all x2 -> x0, waiting for transfers between devices: 140 us -> none  [the longest x1 102 us: body(): lax.all_to_all(homeward, 'fsdp', split_axis=2, concat_axis=2, tiled=True)]
    all_to_all x0 -> x3, blocking collectives: none -> 128 us  [the longest x1 70 us: body(): lax.all_to_all(outgoing, 'fsdp', split_axis=0, concat_axis=0, tiled=True)]
    reduce_scatter x1 -> x0, waiting for transfers between devices: 48.1 us -> none  [body(): lax.psum_scatter(grad_parts.astype(jnp.float32).astype(jnp.bfloat16), 'dp...]
    all_to_all x2 -> x0, starting transfers between devices: 45.9 us -> none  [the longest x1 22.9 us: body(): lax.all_to_all(outgoing, 'fsdp', split_axis=1, concat_axis=1, tiled=True)]
    all_gather x1 -> x0, waiting for transfers between devices: 21.7 us -> none  [body(): every_group = lax.all_gather(direction[None], 'dp', axis=0, tiled=True)]
    all_gather x0 -> x1, blocking collectives: none -> 12.8 us  [body(): gathered = lax.all_gather(picked, 'dp', axis=0, tiled=True)]
    dot_general x11 -> x0, matrix products: 9.31 us -> none  [the longest x8 8.32 us: batched_product(): jnp.einsum('sij,sjk->sik', first_term, second_term, precision=lax.Precisi...]
    pallas_call x0 -> x3, Pallas kernels: none -> 4.85 us  [the longest x1 3.07 us: body(): pl.pallas_call(precondition_kernel, out_shape=(wire, jax.ShapeDtypeStruct...]
  transfers between devices with their start and end apart: 4 -> 0, of which waited for: 4 -> 0; matrix products, arithmetic and copies ran while one was open for 2% -> 0% of each run, Pallas kernels for 0% -> 0%
where the time goes in v1:
time: 148 us
  blocking collectives  141 us (95%)
  Pallas kernels  4.85 us (3%)
    all_to_all x1, blocking collectives, body(): lax.all_to_all(outgoing, 'fsdp', split_axis=0, concat_axis=0, tiled=True)  70 us
    all_to_all x1, blocking collectives, body(): lax.all_to_all(directions, 'fsdp', split_axis=0, concat_axis=0, tiled=True)  44.1 us
    all_to_all x1, blocking collectives, body(): parts = lax.all_to_all(mine, 'dp', split_axis=0, concat_axis=0, tiled=True)  14.1 us
    all_gather x1, blocking collectives, body(): gathered = lax.all_gather(picked, 'dp', axis=0, tiled=True)  12.8 us
    pallas_call x1, Pallas kernels, body(): pl.pallas_call(precondition_kernel, out_shape=(wire, jax.ShapeDtypeStruct...  3.07 us

profile of v1, /device:TPU:6, one launch (start us, length us, event | category | flops | bytes accessed | tf_op | source)
XLA Modules:
  0.0 147.9 jit_solution(6627005074449408469)
XLA Ops:
  0.6 0.0 copy-start
  0.6 14.1 %all_to_all.15.parts = bf16[4,32,8,256]{3,2,1,0:T(8,128)(2,1)S(1)} all-to-all(bf16[4,32,8,256]{3,2,1,0:T(8,128)(2,1)} %bitcast.8), channel_id=1, replica_groups=mesh['fsdp'=32,'dp'=4,'mp'=8] {'dp'}, dimensions={0} | all-to-all | bytes 1048576 | tf_op jit(solution)/shard_map/all_to_all | solution.py:124
  14.7 0.0 copy-start.1
  14.7 0.7 copy-done.1
  15.4 0.9 sum_and_place.1
  16.3 70.0 %all_to_all.16.rows = bf16[32,2,8,256]{3,2,1,0:T(8,128)(2,1)S(1)} all-to-all(bf16[32,2,8,256]{3,2,1,0:T(8,128)(2,1)S(1)} %sum_and_place.1), channel_id=1, replica_groups=mesh['fsdp'=32,'dp'=4,'mp'=8] {'fsdp'}, dimensions={0} | all-to-all | bytes 524288 | tf_op jit(solution)/shard_map/all_to_all | solution.py:134
  86.3 0.0 copy-done
  86.3 3.1 %precondition.1 = (bf16[32,2,8,256]{3,2,1,0:T(8,128)(2,1)S(1)}, f32[2,2,256,256]{3,2,1,0:T(8,128)}) custom-call(s32[128]{0:T(128)S(1)} %bitcast.6, bf16[32,2,8,256]{3,2,1,0:T(8,128)(2,1)S(1)} %all_to_all.16.rows, f32[2,2,256,256]{3,2,1,0:T(8,128)S(1)} %bitcast.4), custom_call_target="tpu_custom_call" | custom-call | tf_op jit(solution)/shard_map/precondition/pallas_call | solution.py:135
  89.4 44.1 %all_to_all.17.rows = bf16[32,2,8,256]{3,2,1,0:T(8,128)(2,1)S(1)} all-to-all(bf16[32,2,8,256]{3,2,1,0:T(8,128)(2,1)S(1)} %get-tuple-element.4), channel_id=1, replica_groups=mesh['fsdp'=32,'dp'=4,'mp'=8] {'fsdp'}, dimensions={0} | all-to-all | bytes 524288 | tf_op jit(solution)/shard_map/all_to_all | solution.py:143
  133.4 0.9 pick.1
  134.3 12.8 %all_gather.3 = bf16[128,8,256]{2,1,0:T(8,128)(2,1)S(1)} all-gather(bf16[32,8,256]{2,1,0:T(8,128)(2,1)S(1)} %pick.1), channel_id=1, replica_groups=mesh['fsdp'=32,'dp'=4,'mp'=8] {'dp'}, dimensions={0}, use_global_device_ids=true | all-gather | bytes 655360 | tf_op jit(solution)/shard_map/all_gather | solution.py:153
  147.1 0.8 copy.6
Async XLA Ops:
  0.6 85.7 %copy-start = (f32[1,1,2,2,256,256]{5,4,3,2,1,0:T(8,128)S(1)}, f32[1,1,2,2,256,256]{5,4,3,2,1,0:T(8,128)}, u32[]{:S(2)}) copy-start(f32[1,1,2,2,256,256]{5,4,3,2,1,0:T(8,128)} %param.5) | copy-start | bytes 3145732
  14.7 0.7 copy-start.1

commit v2 on v1

v2 whole, which is shorter than its diff:
```python
import numpy as np
import jax
import jax.numpy as jnp
from jax import lax
from jax.experimental import pallas as pl
from jax.experimental.pallas import tpu as pltpu
from jax.sharding import PartitionSpec as P

decay_rate = 0.95
epsilon = 1e-06
centre = 0.5


def root_coefficients():
    x = np.polynomial.Polynomial([centre, 1.0])
    t0 = (5.0 - x) / 4.0
    t1 = (5.0 - t0**4 * x) / 4.0
    return [float(c) for c in (t0 * t1).coef]


def dot(a, b, contract):
    return lax.dot_general(a, b, ((contract[:1], contract[1:]), ((), ())), preferred_element_type=jnp.float32)


def mean_square(x):
    return jnp.sum(jnp.sum(x * x, axis=0, keepdims=True), axis=1, keepdims=True) / x.size


def next_place(owners, seen, b):
    owner = owners[b]
    slot = seen[owner]
    seen[owner] = slot + 1
    return owner, slot


def place_kernel(owners_hbm, parts, out, owners, seen, total, sem):
    fetch = pltpu.make_async_copy(owners_hbm, owners, sem)
    fetch.start()
    replicas, count = parts.shape[:2]
    for b in range(count):
        row_sum = parts[0, b].astype(jnp.float32)
        for r in range(1, replicas):
            row_sum = row_sum + parts[r, b].astype(jnp.float32)
        total[b] = row_sum.astype(total.dtype)
    out[...] = jnp.zeros_like(out)
    for i in range(out.shape[0]):
        seen[i] = 0
    first = lax.axis_index("dp") * count
    fetch.wait()
    for b in range(count):
        owner, slot = next_place(owners, seen, first + b)
        out[owner, slot] = total[b]


def pick_kernel(owners, rows, out, seen):
    replicas, count = out.shape[:2]
    for i in range(rows.shape[0]):
        seen[i] = 0
    first = lax.axis_index("dp") * count
    for b in range(count):
        owner, slot = next_place(owners, seen, first + b)
        block = rows[owner, slot]
        for r in range(replicas):
            out[r, b] = block


def precondition_kernel(owners, rows, factors, out, state):
    count, slots = rows.shape[:2]
    order = factors.shape[-1]
    first = lax.axis_index("dp") * count
    me = lax.axis_index("fsdp")
    live = jnp.int32(0)
    for b in range(count):
        live = live + jnp.where(owners[first + b] == me, 1, 0)
    r = root_coefficients()
    half_type = jnp.bfloat16
    diagonal = lax.broadcasted_iota(jnp.int32, (order, order), 0) == lax.broadcasted_iota(
        jnp.int32, (order, order), 1
    )
    wide = [rows[:, s].astype(jnp.float32).reshape(order, order) for s in range(slots)]
    g = [w.astype(half_type) for w in wide]
    pairs = [(s, side) for s in range(slots) for side in range(2)]
    factor = []
    for s, side in pairs:
        gram = dot(g[s], g[s], (1, 1) if side == 0 else (0, 0))
        factor.append(decay_rate * factors[s, side] + gram)
        state[s, side] = jnp.where(s < live, factor[-1], factors[s, side])
    bound = [jnp.max(jnp.sum(jnp.abs(a), axis=0, keepdims=True), axis=1, keepdims=True) + epsilon for a in factor]
    m = [a * (1.0 / c) - jnp.where(diagonal, centre, 0.0) for a, c in zip(factor, bound)]
    mh = [x.astype(half_type) for x in m]
    m2 = [dot(x, x, (1, 0)) for x in mh]
    m2h = [x.astype(half_type) for x in m2]
    u = [(r[5] * x + r[6] * y).astype(half_type) for x, y in zip(m, m2)]
    w = [dot(x, y, (1, 0)) for x, y in zip(m2h, u)]
    v = [(r[3] * x + r[4] * y + z).astype(half_type) for x, y, z in zip(m, m2, w)]
    p = [dot(x, y, (1, 0)) for x, y in zip(m2h, v)]
    root = [
        (jnp.where(diagonal, r[0], 0.0) + r[1] * x + r[2] * y + z).astype(half_type) for x, y, z in zip(m, m2, p)
    ]
    for s in range(slots):
        half = dot(root[2 * s], g[s], (1, 0)).astype(half_type)
        raw = dot(half, root[2 * s + 1], (1, 0))
        ratio = jnp.sqrt(mean_square(wide[s]) + epsilon) / jnp.sqrt(mean_square(raw) + epsilon)
        out[:, s] = (raw * ratio).reshape(count, rows.shape[2], order).astype(out.dtype)


def body(grad_parts, owner_ids, factors):
    fsdp_count = lax.axis_size("fsdp")
    replica_count = lax.axis_size("dp")
    slot_count = factors.shape[2]
    row_count, width = grad_parts.shape[2:]
    group_blocks = grad_parts.shape[1] // replica_count
    owners = owner_ids.reshape(-1)
    vmem = pl.BlockSpec(memory_space=pltpu.VMEM)
    smem = pl.BlockSpec(memory_space=pltpu.SMEM)
    seen = pltpu.SMEM((fsdp_count,), jnp.int32)
    params = pltpu.CompilerParams(vmem_limit_bytes=32 * 1024 * 1024)
    wire = jax.ShapeDtypeStruct((fsdp_count, slot_count, row_count, width), jnp.bfloat16)

    mine = grad_parts.reshape(replica_count, group_blocks, row_count, width)
    parts = lax.all_to_all(mine, "dp", split_axis=0, concat_axis=0, tiled=True)
    outgoing = pl.pallas_call(
        place_kernel,
        out_shape=wire,
        in_specs=[pl.BlockSpec(memory_space=pltpu.HBM), vmem],
        out_specs=vmem,
        scratch_shapes=[
            pltpu.SMEM(owners.shape, jnp.int32),
            seen,
            pltpu.VMEM(mine.shape[1:], jnp.bfloat16),
            pltpu.SemaphoreType.DMA,
        ],
        compiler_params=params,
        name="sum_and_place",
    )(pltpu.with_memory_space_constraint(owners, pltpu.HBM), parts)
    arrived = lax.all_to_all(outgoing, "fsdp", split_axis=0, concat_axis=0, tiled=True)
    directions, state = pl.pallas_call(
        precondition_kernel,
        out_shape=(wire, jax.ShapeDtypeStruct(factors.shape[2:], factors.dtype)),
        in_specs=[smem, vmem, vmem],
        out_specs=(vmem, vmem),
        compiler_params=params,
        name="precondition",
    )(owners, arrived, factors[0, 0])
    returned = lax.all_to_all(directions, "fsdp", split_axis=0, concat_axis=0, tiled=True)
    picked = pl.pallas_call(
        pick_kernel,
        out_shape=jax.ShapeDtypeStruct(mine.shape, jnp.bfloat16),
        in_specs=[smem, vmem],
        out_specs=vmem,
        scratch_shapes=[seen],
        compiler_params=params,
        name="pick",
    )(owners, returned)
    gathered = lax.all_to_all(picked, "dp", split_axis=0, concat_axis=0, tiled=True)
    return gathered.reshape(grad_parts.shape[1:]), state[None, None]


def solution(mesh):
    return jax.shard_map(
        body,
        mesh=mesh,
        in_specs=(
            P("dp", "mp", "fsdp", None),
            P("mp", None),
            P("mp", "dp", "fsdp", None, None, None),
        ),
        out_specs=(P("mp", "fsdp", None), P("mp", "dp", "fsdp", None, None, None)),
        check_vma=False,
    )
```

time: 148 us -> 145 us (0.980)
  blocking collectives: 141 us -> 139 us
    all_gather x1 -> x0, blocking collectives: 12.8 us -> none  [body(): gathered = lax.all_gather(picked, 'dp', axis=0, tiled=True)]
    all_to_all x0 -> x1, blocking collectives: none -> 10.5 us  [body(): lax.all_to_all(picked, 'dp', split_axis=0, concat_axis=0, tiled=True)]
where the time goes in v2:
time: 145 us; the launch traced here: 144 us
  blocking collectives  139 us (96%)
  Pallas kernels  3.64 us (3%)
  local copies, waits for them, and re-layouts  1.45 us (1%)
    all_to_all x1, blocking collectives, body(): lax.all_to_all(outgoing, 'fsdp', split_axis=0, concat_axis=0, tiled=True)  70 us
    all_to_all x1, blocking collectives, body(): lax.all_to_all(directions, 'fsdp', split_axis=0, concat_axis=0, tiled=True)  44.1 us
    all_to_all x1, blocking collectives, body(): parts = lax.all_to_all(mine, 'dp', split_axis=0, concat_axis=0, tiled=True)  14.1 us
    all_to_all x1, blocking collectives, body(): lax.all_to_all(picked, 'dp', split_axis=0, concat_axis=0, tiled=True)  10.5 us

profile of v2, /device:TPU:6, one launch (start us, length us, event | category | flops | bytes accessed | tf_op | source)
XLA Modules:
  0.0 144.4 jit_solution(11902010119546595386)
XLA Ops:
  0.6 0.0 copy-start
  0.6 14.1 %all_to_all.20.parts = bf16[4,32,8,256]{3,2,1,0:T(8,128)(2,1)S(1)} all-to-all(bf16[4,32,8,256]{3,2,1,0:T(8,128)(2,1)} %bitcast.10), channel_id=1, replica_groups=mesh['fsdp'=32,'dp'=4,'mp'=8] {'dp'}, dimensions={0} | all-to-all | bytes 1048576 | tf_op jit(solution)/shard_map/all_to_all | solution.py:121
  14.7 0.8 sum_and_place.1
  15.5 70.0 %all_to_all.21.rows = bf16[32,2,8,256]{3,2,1,0:T(8,128)(2,1)S(1)} all-to-all(bf16[32,2,8,256]{3,2,1,0:T(8,128)(2,1)S(1)} %sum_and_place.1), channel_id=1, replica_groups=mesh['fsdp'=32,'dp'=4,'mp'=8] {'fsdp'}, dimensions={0} | all-to-all | bytes 524288 | tf_op jit(solution)/shard_map/all_to_all | solution.py:136
  85.5 0.0 copy-start.1
  85.5 0.0 copy-done
  85.5 0.7 copy-done.1
  86.2 2.1 %precondition.1 = (bf16[32,2,8,256]{3,2,1,0:T(8,128)(2,1)S(1)}, f32[2,2,256,256]{3,2,1,0:T(8,128)}) custom-call(s32[128]{0:T(128)S(1)} %bitcast.7, bf16[32,2,8,256]{3,2,1,0:T(8,128)(2,1)S(1)} %all_to_all.21.rows, f32[2,2,256,256]{3,2,1,0:T(8,128)S(1)} %bitcast.5), custom_call_target="tpu_custom_call" | custom-call | tf_op jit(solution)/shard_map/precondition/pallas_call | solution.py:137
  88.3 44.1 %all_to_all.22.rows = bf16[32,2,8,256]{3,2,1,0:T(8,128)(2,1)S(1)} all-to-all(bf16[32,2,8,256]{3,2,1,0:T(8,128)(2,1)S(1)} %get-tuple-element.4), channel_id=1, replica_groups=mesh['fsdp'=32,'dp'=4,'mp'=8] {'fsdp'}, dimensions={0} | all-to-all | bytes 524288 | tf_op jit(solution)/shard_map/all_to_all | solution.py:145
  132.4 0.7 pick.1
  133.1 10.5 %all_to_all.23 = bf16[4,32,8,256]{3,2,1,0:T(8,128)(2,1)S(1)} all-to-all(bf16[4,32,8,256]{3,2,1,0:T(8,128)(2,1)S(1)} %pick.1), channel_id=1, replica_groups=mesh['fsdp'=32,'dp'=4,'mp'=8] {'dp'}, dimensions={0} | all-to-all | bytes 1048576 | tf_op jit(solution)/shard_map/all_to_all | solution.py:155
  143.6 0.8 copy.6
Async XLA Ops:
  0.6 84.9 %copy-start = (f32[1,1,2,2,256,256]{5,4,3,2,1,0:T(8,128)S(1)}, f32[1,1,2,2,256,256]{5,4,3,2,1,0:T(8,128)}, u32[]{:S(2)}) copy-start(f32[1,1,2,2,256,256]{5,4,3,2,1,0:T(8,128)} %param.5) | copy-start | bytes 3145732
  85.5 0.7 copy-start.1

commit v3 on v2

--- a/solution.py
+++ b/solution.py
@@ -26,14 +26,7 @@
     return jnp.sum(jnp.sum(x * x, axis=0, keepdims=True), axis=1, keepdims=True) / x.size
 
 
-def next_place(owners, seen, b):
-    owner = owners[b]
-    slot = seen[owner]
-    seen[owner] = slot + 1
-    return owner, slot
-
-
-def place_kernel(owners_hbm, parts, out, owners, seen, total, sem):
+def place_kernel(owners_hbm, parts, out, places, owners, seen, total, sem):
     fetch = pltpu.make_async_copy(owners_hbm, owners, sem)
     fetch.start()
     replicas, count = parts.shape[:2]
@@ -48,30 +41,29 @@
     first = lax.axis_index("dp") * count
     fetch.wait()
     for b in range(count):
-        owner, slot = next_place(owners, seen, first + b)
+        owner = owners[first + b]
+        slot = seen[owner]
+        seen[owner] = slot + 1
+        places[b] = owner * out.shape[1] + slot
         out[owner, slot] = total[b]
 
 
-def pick_kernel(owners, rows, out, seen):
+def pick_kernel(places, rows, out):
     replicas, count = out.shape[:2]
-    for i in range(rows.shape[0]):
-        seen[i] = 0
-    first = lax.axis_index("dp") * count
+    slots = rows.shape[1]
     for b in range(count):
-        owner, slot = next_place(owners, seen, first + b)
-        block = rows[owner, slot]
+        block = rows[places[b] // slots, places[b] % slots]
         for r in range(replicas):
             out[r, b] = block
 
 
-def precondition_kernel(owners, rows, factors, out, state):
+def precondition_kernel(places, rows, factors, out, state):
     count, slots = rows.shape[:2]
     order = factors.shape[-1]
-    first = lax.axis_index("dp") * count
     me = lax.axis_index("fsdp")
     live = jnp.int32(0)
     for b in range(count):
-        live = live + jnp.where(owners[first + b] == me, 1, 0)
+        live = live + jnp.where(places[b] // slots == me, 1, 0)
     r = root_coefficients()
     half_type = jnp.bfloat16
     diagonal = lax.broadcasted_iota(jnp.int32, (order, order), 0) == lax.broadcasted_iota(
@@ -113,20 +105,19 @@
     owners = owner_ids.reshape(-1)
     vmem = pl.BlockSpec(memory_space=pltpu.VMEM)
     smem = pl.BlockSpec(memory_space=pltpu.SMEM)
-    seen = pltpu.SMEM((fsdp_count,), jnp.int32)
     params = pltpu.CompilerParams(vmem_limit_bytes=32 * 1024 * 1024)
     wire = jax.ShapeDtypeStruct((fsdp_count, slot_count, row_count, width), jnp.bfloat16)
 
     mine = grad_parts.reshape(replica_count, group_blocks, row_count, width)
     parts = lax.all_to_all(mine, "dp", split_axis=0, concat_axis=0, tiled=True)
-    outgoing = pl.pallas_call(
+    outgoing, places = pl.pallas_call(
         place_kernel,
-        out_shape=wire,
+        out_shape=(wire, jax.ShapeDtypeStruct((group_blocks,), jnp.int32)),
         in_specs=[pl.BlockSpec(memory_space=pltpu.HBM), vmem],
-        out_specs=vmem,
+        out_specs=(vmem, smem),
         scratch_shapes=[
             pltpu.SMEM(owners.shape, jnp.int32),
-            seen,
+            pltpu.SMEM((fsdp_count,), jnp.int32),
             pltpu.VMEM(mine.shape[1:], jnp.bfloat16),
             pltpu.SemaphoreType.DMA,
         ],
@@ -141,17 +132,16 @@
         out_specs=(vmem, vmem),
         compiler_params=params,
         name="precondition",
-    )(owners, arrived, factors[0, 0])
+    )(places, arrived, factors[0, 0])
     returned = lax.all_to_all(directions, "fsdp", split_axis=0, concat_axis=0, tiled=True)
     picked = pl.pallas_call(
         pick_kernel,
         out_shape=jax.ShapeDtypeStruct(mine.shape, jnp.bfloat16),
         in_specs=[smem, vmem],
         out_specs=vmem,
-        scratch_shapes=[seen],
         compiler_params=params,
         name="pick",
-    )(owners, returned)
+    )(places, returned)
     gathered = lax.all_to_all(picked, "dp", split_axis=0, concat_axis=0, tiled=True)
     return gathered.reshape(grad_parts.shape[1:]), state[None, None]
 

time: 145 us -> 145 us (level)
  no operation moved by 1% of the time
where the time goes in v3:
time: 145 us; the launch traced here: 144 us
  blocking collectives  139 us (96%)
  Pallas kernels  4.34 us (3%)
    all_to_all x1, blocking collectives, body(): lax.all_to_all(outgoing, 'fsdp', split_axis=0, concat_axis=0, tiled=True)  70 us
    all_to_all x1, blocking collectives, body(): lax.all_to_all(directions, 'fsdp', split_axis=0, concat_axis=0, tiled=True)  44.1 us
    all_to_all x1, blocking collectives, body(): parts = lax.all_to_all(mine, 'dp', split_axis=0, concat_axis=0, tiled=True)  14.1 us
    all_to_all x1, blocking collectives, body(): lax.all_to_all(picked, 'dp', split_axis=0, concat_axis=0, tiled=True)  10.5 us

profile of v3, /device:TPU:6, one launch (start us, length us, event | category | flops | bytes accessed | tf_op | source)
XLA Modules:
  0.0 144.4 jit_solution(1892804619615375238)
XLA Ops:
  0.6 0.0 copy-start
  0.6 14.1 %all_to_all.20.parts = bf16[4,32,8,256]{3,2,1,0:T(8,128)(2,1)S(1)} all-to-all(bf16[4,32,8,256]{3,2,1,0:T(8,128)(2,1)} %bitcast.7), channel_id=1, replica_groups=mesh['fsdp'=32,'dp'=4,'mp'=8] {'dp'}, dimensions={0} | all-to-all | bytes 1048576 | tf_op jit(solution)/shard_map/all_to_all | solution.py:112
  14.7 1.4 sum_and_place.1
  16.1 70.0 %all_to_all.21.rows = bf16[32,2,8,256]{3,2,1,0:T(8,128)(2,1)S(1)} all-to-all(bf16[32,2,8,256]{3,2,1,0:T(8,128)(2,1)S(1)} %get-tuple-element.7), channel_id=1, replica_groups=mesh['fsdp'=32,'dp'=4,'mp'=8] {'fsdp'}, dimensions={0} | all-to-all | bytes 524288 | tf_op jit(solution)/shard_map/all_to_all | solution.py:127
  86.1 0.0 copy-done
  86.1 2.2 %precondition.1 = (bf16[32,2,8,256]{3,2,1,0:T(8,128)(2,1)S(1)}, f32[2,2,256,256]{3,2,1,0:T(8,128)}) custom-call(s32[32]{0:T(128)S(1)} %get-tuple-element.6.places, bf16[32,2,8,256]{3,2,1,0:T(8,128)(2,1)S(1)} %all_to_all.21.rows, f32[2,2,256,256]{3,2,1,0:T(8,128)S(1)} %bitcast.5), custom_call_target="tpu_custom_call" | custom-call | tf_op jit(solution)/shard_map/precondition/pallas_call | solution.py:128
  88.3 44.1 %all_to_all.22.rows = bf16[32,2,8,256]{3,2,1,0:T(8,128)(2,1)S(1)} all-to-all(bf16[32,2,8,256]{3,2,1,0:T(8,128)(2,1)S(1)} %get-tuple-element.8), channel_id=1, replica_groups=mesh['fsdp'=32,'dp'=4,'mp'=8] {'fsdp'}, dimensions={0} | all-to-all | bytes 524288 | tf_op jit(solution)/shard_map/all_to_all | solution.py:136
  132.4 0.8 pick.1
  133.2 10.5 %all_to_all.23 = bf16[4,32,8,256]{3,2,1,0:T(8,128)(2,1)S(1)} all-to-all(bf16[4,32,8,256]{3,2,1,0:T(8,128)(2,1)S(1)} %pick.1), channel_id=1, replica_groups=mesh['fsdp'=32,'dp'=4,'mp'=8] {'dp'}, dimensions={0} | all-to-all | bytes 1048576 | tf_op jit(solution)/shard_map/all_to_all | solution.py:145
  143.6 0.8 copy.6
Async XLA Ops:
  0.6 85.5 %copy-start = (f32[1,1,2,2,256,256]{5,4,3,2,1,0:T(8,128)S(1)}, f32[1,1,2,2,256,256]{5,4,3,2,1,0:T(8,128)}, u32[]{:S(2)}) copy-start(f32[1,1,2,2,256,256]{5,4,3,2,1,0:T(8,128)} %param.5) | copy-start | bytes 3145732

commit v4 on v2

--- a/solution.py
+++ b/solution.py
@@ -33,9 +33,11 @@
     return owner, slot
 
 
-def place_kernel(owners_hbm, parts, out, owners, seen, total, sem):
-    fetch = pltpu.make_async_copy(owners_hbm, owners, sem)
+def place_kernel(owners_hbm, parts, out, kept_owners, owners, seen, total, sem):
+    fetch = pltpu.make_async_copy(owners_hbm, owners, sem.at[0])
     fetch.start()
+    keep = pltpu.make_async_copy(owners_hbm, kept_owners, sem.at[1])
+    keep.start()
     replicas, count = parts.shape[:2]
     for b in range(count):
         row_sum = parts[0, b].astype(jnp.float32)
@@ -50,6 +52,7 @@
     for b in range(count):
         owner, slot = next_place(owners, seen, first + b)
         out[owner, slot] = total[b]
+    keep.wait()
 
 
 def pick_kernel(owners, rows, out, seen):
@@ -119,16 +122,16 @@
 
     mine = grad_parts.reshape(replica_count, group_blocks, row_count, width)
     parts = lax.all_to_all(mine, "dp", split_axis=0, concat_axis=0, tiled=True)
-    outgoing = pl.pallas_call(
+    outgoing, kept_owners = pl.pallas_call(
         place_kernel,
-        out_shape=wire,
+        out_shape=(wire, pltpu.VMEM(owners.shape, jnp.int32)),
         in_specs=[pl.BlockSpec(memory_space=pltpu.HBM), vmem],
-        out_specs=vmem,
+        out_specs=(vmem, vmem),
         scratch_shapes=[
             pltpu.SMEM(owners.shape, jnp.int32),
             seen,
             pltpu.VMEM(mine.shape[1:], jnp.bfloat16),
-            pltpu.SemaphoreType.DMA,
+            pltpu.SemaphoreType.DMA((2,)),
         ],
         compiler_params=params,
         name="sum_and_place",
@@ -141,7 +144,7 @@
         out_specs=(vmem, vmem),
         compiler_params=params,
         name="precondition",
-    )(owners, arrived, factors[0, 0])
+    )(kept_owners, arrived, factors[0, 0])
     returned = lax.all_to_all(directions, "fsdp", split_axis=0, concat_axis=0, tiled=True)
     picked = pl.pallas_call(
         pick_kernel,
@@ -151,7 +154,7 @@
         scratch_shapes=[seen],
         compiler_params=params,
         name="pick",
-    )(owners, returned)
+    )(kept_owners, returned)
     gathered = lax.all_to_all(picked, "dp", split_axis=0, concat_axis=0, tiled=True)
     return gathered.reshape(grad_parts.shape[1:]), state[None, None]
 

time: 145 us -> 144 us (level)
  no operation moved by 1% of the time
where the time goes in v4:
time: 144 us
  blocking collectives  139 us (97%)
  Pallas kernels  3.65 us (3%)
    all_to_all x1, blocking collectives, body(): lax.all_to_all(outgoing, 'fsdp', split_axis=0, concat_axis=0, tiled=True)  70 us
    all_to_all x1, blocking collectives, body(): lax.all_to_all(directions, 'fsdp', split_axis=0, concat_axis=0, tiled=True)  44.1 us
    all_to_all x1, blocking collectives, body(): parts = lax.all_to_all(mine, 'dp', split_axis=0, concat_axis=0, tiled=True)  14.1 us
    all_to_all x1, blocking collectives, body(): lax.all_to_all(picked, 'dp', split_axis=0, concat_axis=0, tiled=True)  10.5 us

profile of v4, /device:TPU:6, one launch (start us, length us, event | category | flops | bytes accessed | tf_op | source)
XLA Modules:
  0.0 143.7 jit_solution(369822938074616529)
XLA Ops:
  0.6 0.0 copy-start
  0.6 14.1 %all_to_all.20.parts = bf16[4,32,8,256]{3,2,1,0:T(8,128)(2,1)S(1)} all-to-all(bf16[4,32,8,256]{3,2,1,0:T(8,128)(2,1)} %bitcast.7), channel_id=1, replica_groups=mesh['fsdp'=32,'dp'=4,'mp'=8] {'dp'}, dimensions={0} | all-to-all | bytes 1048576 | tf_op jit(solution)/shard_map/all_to_all | solution.py:124
  14.7 0.8 sum_and_place.1
  15.6 70.0 %all_to_all.21.rows = bf16[32,2,8,256]{3,2,1,0:T(8,128)(2,1)S(1)} all-to-all(bf16[32,2,8,256]{3,2,1,0:T(8,128)(2,1)S(1)} %get-tuple-element.7), channel_id=1, replica_groups=mesh['fsdp'=32,'dp'=4,'mp'=8] {'fsdp'}, dimensions={0} | all-to-all | bytes 524288 | tf_op jit(solution)/shard_map/all_to_all | solution.py:139
  85.5 0.0 copy-done
  85.5 2.1 %precondition.1 = (bf16[32,2,8,256]{3,2,1,0:T(8,128)(2,1)S(1)}, f32[2,2,256,256]{3,2,1,0:T(8,128)}) custom-call(s32[128]{0:T(128)S(1)} %get-tuple-element.6.owners, bf16[32,2,8,256]{3,2,1,0:T(8,128)(2,1)S(1)} %all_to_all.21.rows, f32[2,2,256,256]{3,2,1,0:T(8,128)S(1)} %bitcast.5), custom_call_target="tpu_custom_call" | custom-call | tf_op jit(solution)/shard_map/precondition/pallas_call | solution.py:140
  87.7 44.1 %all_to_all.22.rows = bf16[32,2,8,256]{3,2,1,0:T(8,128)(2,1)S(1)} all-to-all(bf16[32,2,8,256]{3,2,1,0:T(8,128)(2,1)S(1)} %get-tuple-element.8), channel_id=1, replica_groups=mesh['fsdp'=32,'dp'=4,'mp'=8] {'fsdp'}, dimensions={0} | all-to-all | bytes 524288 | tf_op jit(solution)/shard_map/all_to_all | solution.py:148
  131.8 0.7 pick.1
  132.5 10.5 %all_to_all.23 = bf16[4,32,8,256]{3,2,1,0:T(8,128)(2,1)S(1)} all-to-all(bf16[4,32,8,256]{3,2,1,0:T(8,128)(2,1)S(1)} %pick.1), channel_id=1, replica_groups=mesh['fsdp'=32,'dp'=4,'mp'=8] {'dp'}, dimensions={0} | all-to-all | bytes 1048576 | tf_op jit(solution)/shard_map/all_to_all | solution.py:158
  143.0 0.8 copy.6
Async XLA Ops:
  0.6 84.9 %copy-start = (f32[1,1,2,2,256,256]{5,4,3,2,1,0:T(8,128)S(1)}, f32[1,1,2,2,256,256]{5,4,3,2,1,0:T(8,128)}, u32[]{:S(2)}) copy-start(f32[1,1,2,2,256,256]{5,4,3,2,1,0:T(8,128)} %param.5) | copy-start | bytes 3145732

commit v5 on v4

--- a/solution.py
+++ b/solution.py
@@ -33,7 +33,7 @@
     return owner, slot
 
 
-def place_kernel(owners_hbm, parts, out, kept_owners, owners, seen, total, sem):
+def place_kernel(owners_hbm, parts, out, kept_owners, used, owners, seen, total, sem):
     fetch = pltpu.make_async_copy(owners_hbm, owners, sem.at[0])
     fetch.start()
     keep = pltpu.make_async_copy(owners_hbm, kept_owners, sem.at[1])
@@ -52,6 +52,9 @@
     for b in range(count):
         owner, slot = next_place(owners, seen, first + b)
         out[owner, slot] = total[b]
+    live = seen[lax.axis_index("fsdp")]
+    for s in range(used.shape[0]):
+        used[s : s + 1, :] = jnp.full((1, used.shape[1]), jnp.where(s < live, 1.0, 0.0), used.dtype)
     keep.wait()
 
 
@@ -67,14 +70,9 @@
             out[r, b] = block
 
 
-def precondition_kernel(owners, rows, factors, out, state):
+def precondition_kernel(used, rows, factors, out, state):
     count, slots = rows.shape[:2]
     order = factors.shape[-1]
-    first = lax.axis_index("dp") * count
-    me = lax.axis_index("fsdp")
-    live = jnp.int32(0)
-    for b in range(count):
-        live = live + jnp.where(owners[first + b] == me, 1, 0)
     r = root_coefficients()
     half_type = jnp.bfloat16
     diagonal = lax.broadcasted_iota(jnp.int32, (order, order), 0) == lax.broadcasted_iota(
@@ -87,7 +85,7 @@
     for s, side in pairs:
         gram = dot(g[s], g[s], (1, 1) if side == 0 else (0, 0))
         factor.append(decay_rate * factors[s, side] + gram)
-        state[s, side] = jnp.where(s < live, factor[-1], factors[s, side])
+        state[s, side] = jnp.where(used[s : s + 1, :] > 0.0, factor[-1], factors[s, side])
     bound = [jnp.max(jnp.sum(jnp.abs(a), axis=0, keepdims=True), axis=1, keepdims=True) + epsilon for a in factor]
     m = [a * (1.0 / c) - jnp.where(diagonal, centre, 0.0) for a, c in zip(factor, bound)]
     mh = [x.astype(half_type) for x in m]
@@ -122,11 +120,15 @@
 
     mine = grad_parts.reshape(replica_count, group_blocks, row_count, width)
     parts = lax.all_to_all(mine, "dp", split_axis=0, concat_axis=0, tiled=True)
-    outgoing, kept_owners = pl.pallas_call(
+    outgoing, kept_owners, used = pl.pallas_call(
         place_kernel,
-        out_shape=(wire, pltpu.VMEM(owners.shape, jnp.int32)),
+        out_shape=(
+            wire,
+            pltpu.VMEM(owners.shape, jnp.int32),
+            pltpu.VMEM((slot_count, factors.shape[-1]), jnp.float32),
+        ),
         in_specs=[pl.BlockSpec(memory_space=pltpu.HBM), vmem],
-        out_specs=(vmem, vmem),
+        out_specs=(vmem, vmem, vmem),
         scratch_shapes=[
             pltpu.SMEM(owners.shape, jnp.int32),
             seen,
@@ -140,11 +142,11 @@
     directions, state = pl.pallas_call(
         precondition_kernel,
         out_shape=(wire, jax.ShapeDtypeStruct(factors.shape[2:], factors.dtype)),
-        in_specs=[smem, vmem, vmem],
+        in_specs=[vmem, vmem, vmem],
         out_specs=(vmem, vmem),
         compiler_params=params,
         name="precondition",
-    )(kept_owners, arrived, factors[0, 0])
+    )(used, arrived, factors[0, 0])
     returned = lax.all_to_all(directions, "fsdp", split_axis=0, concat_axis=0, tiled=True)
     picked = pl.pallas_call(
         pick_kernel,

time: 144 us -> 143 us (level)
  no operation moved by 1% of the time
where the time goes in v5:
time: 143 us
  blocking collectives  139 us (97%)
  Pallas kernels  3.07 us (2%)
    all_to_all x1, blocking collectives, body(): lax.all_to_all(outgoing, 'fsdp', split_axis=0, concat_axis=0, tiled=True)  70 us
    all_to_all x1, blocking collectives, body(): lax.all_to_all(directions, 'fsdp', split_axis=0, concat_axis=0, tiled=True)  44.1 us
    all_to_all x1, blocking collectives, body(): parts = lax.all_to_all(mine, 'dp', split_axis=0, concat_axis=0, tiled=True)  14.1 us
    all_to_all x1, blocking collectives, body(): lax.all_to_all(picked, 'dp', split_axis=0, concat_axis=0, tiled=True)  10.5 us

profile of v5, /device:TPU:6, one launch (start us, length us, event | category | flops | bytes accessed | tf_op | source)
XLA Modules:
  0.0 143.2 jit_solution(5949003253153659054)
XLA Ops:
  0.6 0.0 copy-start
  0.6 14.1 %all_to_all.20.parts = bf16[4,32,8,256]{3,2,1,0:T(8,128)(2,1)S(1)} all-to-all(bf16[4,32,8,256]{3,2,1,0:T(8,128)(2,1)} %bitcast.7), channel_id=1, replica_groups=mesh['fsdp'=32,'dp'=4,'mp'=8] {'dp'}, dimensions={0} | all-to-all | bytes 1048576 | tf_op jit(solution)/shard_map/all_to_all | solution.py:122
  14.7 0.8 sum_and_place.1
  15.6 70.0 %all_to_all.21.rows = bf16[32,2,8,256]{3,2,1,0:T(8,128)(2,1)S(1)} all-to-all(bf16[32,2,8,256]{3,2,1,0:T(8,128)(2,1)S(1)} %get-tuple-element.9), channel_id=1, replica_groups=mesh['fsdp'=32,'dp'=4,'mp'=8] {'fsdp'}, dimensions={0} | all-to-all | bytes 524288 | tf_op jit(solution)/shard_map/all_to_all | solution.py:141
  85.6 0.0 copy-done
  85.6 1.6 %precondition.1 = (bf16[32,2,8,256]{3,2,1,0:T(8,128)(2,1)S(1)}, f32[2,2,256,256]{3,2,1,0:T(8,128)}) custom-call(f32[2,256]{1,0:T(2,128)S(1)} %get-tuple-element.8.used, bf16[32,2,8,256]{3,2,1,0:T(8,128)(2,1)S(1)} %all_to_all.21.rows, f32[2,2,256,256]{3,2,1,0:T(8,128)S(1)} %bitcast.5), custom_call_target="tpu_custom_call" | custom-call | tf_op jit(solution)/shard_map/precondition/pallas_call | solution.py:142
  87.1 44.1 %all_to_all.22.rows = bf16[32,2,8,256]{3,2,1,0:T(8,128)(2,1)S(1)} all-to-all(bf16[32,2,8,256]{3,2,1,0:T(8,128)(2,1)S(1)} %get-tuple-element.10), channel_id=1, replica_groups=mesh['fsdp'=32,'dp'=4,'mp'=8] {'fsdp'}, dimensions={0} | all-to-all | bytes 524288 | tf_op jit(solution)/shard_map/all_to_all | solution.py:150
  131.2 0.7 pick.1
  131.9 10.5 %all_to_all.23 = bf16[4,32,8,256]{3,2,1,0:T(8,128)(2,1)S(1)} all-to-all(bf16[4,32,8,256]{3,2,1,0:T(8,128)(2,1)S(1)} %pick.1), channel_id=1, replica_groups=mesh['fsdp'=32,'dp'=4,'mp'=8] {'dp'}, dimensions={0} | all-to-all | bytes 1048576 | tf_op jit(solution)/shard_map/all_to_all | solution.py:160
  142.4 0.8 copy.6
Async XLA Ops:
  0.6 84.9 %copy-start = (f32[1,1,2,2,256,256]{5,4,3,2,1,0:T(8,128)S(1)}, f32[1,1,2,2,256,256]{5,4,3,2,1,0:T(8,128)}, u32[]{:S(2)}) copy-start(f32[1,1,2,2,256,256]{5,4,3,2,1,0:T(8,128)} %param.5) | copy-start | bytes 3145732

commit v6 on v5

--- a/solution.py
+++ b/solution.py
@@ -33,11 +33,9 @@
     return owner, slot
 
 
-def place_kernel(owners_hbm, parts, out, kept_owners, used, owners, seen, total, sem):
-    fetch = pltpu.make_async_copy(owners_hbm, owners, sem.at[0])
+def place_kernel(owners_hbm, parts, out, owners, used, seen, total, sem):
+    fetch = pltpu.make_async_copy(owners_hbm, owners, sem)
     fetch.start()
-    keep = pltpu.make_async_copy(owners_hbm, kept_owners, sem.at[1])
-    keep.start()
     replicas, count = parts.shape[:2]
     for b in range(count):
         row_sum = parts[0, b].astype(jnp.float32)
@@ -55,7 +53,6 @@
     live = seen[lax.axis_index("fsdp")]
     for s in range(used.shape[0]):
         used[s : s + 1, :] = jnp.full((1, used.shape[1]), jnp.where(s < live, 1.0, 0.0), used.dtype)
-    keep.wait()
 
 
 def pick_kernel(owners, rows, out, seen):
@@ -120,20 +117,19 @@
 
     mine = grad_parts.reshape(replica_count, group_blocks, row_count, width)
     parts = lax.all_to_all(mine, "dp", split_axis=0, concat_axis=0, tiled=True)
-    outgoing, kept_owners, used = pl.pallas_call(
+    outgoing, known_owners, used = pl.pallas_call(
         place_kernel,
         out_shape=(
             wire,
-            pltpu.VMEM(owners.shape, jnp.int32),
+            pltpu.SMEM(owners.shape, jnp.int32),
             pltpu.VMEM((slot_count, factors.shape[-1]), jnp.float32),
         ),
         in_specs=[pl.BlockSpec(memory_space=pltpu.HBM), vmem],
-        out_specs=(vmem, vmem, vmem),
+        out_specs=(vmem, smem, vmem),
         scratch_shapes=[
-            pltpu.SMEM(owners.shape, jnp.int32),
             seen,
             pltpu.VMEM(mine.shape[1:], jnp.bfloat16),
-            pltpu.SemaphoreType.DMA((2,)),
+            pltpu.SemaphoreType.DMA,
         ],
         compiler_params=params,
         name="sum_and_place",
@@ -156,7 +152,7 @@
         scratch_shapes=[seen],
         compiler_params=params,
         name="pick",
-    )(kept_owners, returned)
+    )(known_owners, returned)
     gathered = lax.all_to_all(picked, "dp", split_axis=0, concat_axis=0, tiled=True)
     return gathered.reshape(grad_parts.shape[1:]), state[None, None]
 

time: 143 us -> 143 us (level)
  no operation moved by 1% of the time
where the time goes in v6:
time: 143 us
  blocking collectives  139 us (97%)
  Pallas kernels  2.48 us (2%)
    all_to_all x1, blocking collectives, body(): lax.all_to_all(outgoing, 'fsdp', split_axis=0, concat_axis=0, tiled=True)  70 us
    all_to_all x1, blocking collectives, body(): lax.all_to_all(directions, 'fsdp', split_axis=0, concat_axis=0, tiled=True)  44.1 us
    all_to_all x1, blocking collectives, body(): parts = lax.all_to_all(mine, 'dp', split_axis=0, concat_axis=0, tiled=True)  14.1 us
    all_to_all x1, blocking collectives, body(): lax.all_to_all(picked, 'dp', split_axis=0, concat_axis=0, tiled=True)  10.5 us

profile of v6, /device:TPU:6, one launch (start us, length us, event | category | flops | bytes accessed | tf_op | source)
XLA Modules:
  0.0 142.6 jit_solution(12051278637349527908)
XLA Ops:
  0.6 0.0 copy-start
  0.6 14.1 %all_to_all.20.parts = bf16[4,32,8,256]{3,2,1,0:T(8,128)(2,1)S(1)} all-to-all(bf16[4,32,8,256]{3,2,1,0:T(8,128)(2,1)} %bitcast.7), channel_id=1, replica_groups=mesh['fsdp'=32,'dp'=4,'mp'=8] {'dp'}, dimensions={0} | all-to-all | bytes 1048576 | tf_op jit(solution)/shard_map/all_to_all | solution.py:119
  14.7 0.8 sum_and_place.1
  15.5 70.0 %all_to_all.21.rows = bf16[32,2,8,256]{3,2,1,0:T(8,128)(2,1)S(1)} all-to-all(bf16[32,2,8,256]{3,2,1,0:T(8,128)(2,1)S(1)} %get-tuple-element.9), channel_id=1, replica_groups=mesh['fsdp'=32,'dp'=4,'mp'=8] {'fsdp'}, dimensions={0} | all-to-all | bytes 524288 | tf_op jit(solution)/shard_map/all_to_all | solution.py:137
  85.5 0.0 copy-done
  85.5 1.6 %precondition.1 = (bf16[32,2,8,256]{3,2,1,0:T(8,128)(2,1)S(1)}, f32[2,2,256,256]{3,2,1,0:T(8,128)}) custom-call(f32[2,256]{1,0:T(2,128)S(1)} %get-tuple-element.8.used, bf16[32,2,8,256]{3,2,1,0:T(8,128)(2,1)S(1)} %all_to_all.21.rows, f32[2,2,256,256]{3,2,1,0:T(8,128)S(1)} %bitcast.5), custom_call_target="tpu_custom_call" | custom-call | tf_op jit(solution)/shard_map/precondition/pallas_call | solution.py:138
  87.1 44.1 %all_to_all.22.rows = bf16[32,2,8,256]{3,2,1,0:T(8,128)(2,1)S(1)} all-to-all(bf16[32,2,8,256]{3,2,1,0:T(8,128)(2,1)S(1)} %get-tuple-element.10), channel_id=1, replica_groups=mesh['fsdp'=32,'dp'=4,'mp'=8] {'fsdp'}, dimensions={0} | all-to-all | bytes 524288 | tf_op jit(solution)/shard_map/all_to_all | solution.py:146
  131.2 0.1 pick.1
  131.3 10.5 %all_to_all.23 = bf16[4,32,8,256]{3,2,1,0:T(8,128)(2,1)S(1)} all-to-all(bf16[4,32,8,256]{3,2,1,0:T(8,128)(2,1)S(1)} %pick.1), channel_id=1, replica_groups=mesh['fsdp'=32,'dp'=4,'mp'=8] {'dp'}, dimensions={0} | all-to-all | bytes 1048576 | tf_op jit(solution)/shard_map/all_to_all | solution.py:156
  141.8 0.8 copy.6
Async XLA Ops:
  0.6 84.9 %copy-start = (f32[1,1,2,2,256,256]{5,4,3,2,1,0:T(8,128)S(1)}, f32[1,1,2,2,256,256]{5,4,3,2,1,0:T(8,128)}, u32[]{:S(2)}) copy-start(f32[1,1,2,2,256,256]{5,4,3,2,1,0:T(8,128)} %param.5) | copy-start | bytes 3145732

commit v7 on v6

--- a/solution.py
+++ b/solution.py
@@ -95,11 +95,11 @@
     root = [
         (jnp.where(diagonal, r[0], 0.0) + r[1] * x + r[2] * y + z).astype(half_type) for x, y, z in zip(m, m2, p)
     ]
+    half = [dot(root[2 * s], g[s], (1, 0)).astype(half_type) for s in range(slots)]
+    raw = [dot(half[s], root[2 * s + 1], (1, 0)) for s in range(slots)]
     for s in range(slots):
-        half = dot(root[2 * s], g[s], (1, 0)).astype(half_type)
-        raw = dot(half, root[2 * s + 1], (1, 0))
-        ratio = jnp.sqrt(mean_square(wide[s]) + epsilon) / jnp.sqrt(mean_square(raw) + epsilon)
-        out[:, s] = (raw * ratio).reshape(count, rows.shape[2], order).astype(out.dtype)
+        ratio = jnp.sqrt(mean_square(wide[s]) + epsilon) / jnp.sqrt(mean_square(raw[s]) + epsilon)
+        out[:, s] = (raw[s] * ratio).reshape(count, rows.shape[2], order).astype(out.dtype)
 
 
 def body(grad_parts, owner_ids, factors):

time: 143 us -> 143 us (level)
  no operation moved by 1% of the time
where the time goes in v7:
time: 143 us
  blocking collectives  139 us (97%)
  Pallas kernels  2.46 us (2%)
    all_to_all x1, blocking collectives, body(): lax.all_to_all(outgoing, 'fsdp', split_axis=0, concat_axis=0, tiled=True)  70 us
    all_to_all x1, blocking collectives, body(): lax.all_to_all(directions, 'fsdp', split_axis=0, concat_axis=0, tiled=True)  44.1 us
    all_to_all x1, blocking collectives, body(): parts = lax.all_to_all(mine, 'dp', split_axis=0, concat_axis=0, tiled=True)  14.1 us
    all_to_all x1, blocking collectives, body(): lax.all_to_all(picked, 'dp', split_axis=0, concat_axis=0, tiled=True)  10.5 us

profile of v7, /device:TPU:6, one launch (start us, length us, event | category | flops | bytes accessed | tf_op | source)
XLA Modules:
  0.0 142.6 jit_solution(7517036969823351274)
XLA Ops:
  0.6 0.0 copy-start
  0.6 14.1 %all_to_all.20.parts = bf16[4,32,8,256]{3,2,1,0:T(8,128)(2,1)S(1)} all-to-all(bf16[4,32,8,256]{3,2,1,0:T(8,128)(2,1)} %bitcast.7), channel_id=1, replica_groups=mesh['fsdp'=32,'dp'=4,'mp'=8] {'dp'}, dimensions={0} | all-to-all | bytes 1048576 | tf_op jit(solution)/shard_map/all_to_all | solution.py:119
  14.7 0.8 sum_and_place.1
  15.5 70.0 %all_to_all.21.rows = bf16[32,2,8,256]{3,2,1,0:T(8,128)(2,1)S(1)} all-to-all(bf16[32,2,8,256]{3,2,1,0:T(8,128)(2,1)S(1)} %get-tuple-element.9), channel_id=1, replica_groups=mesh['fsdp'=32,'dp'=4,'mp'=8] {'fsdp'}, dimensions={0} | all-to-all | bytes 524288 | tf_op jit(solution)/shard_map/all_to_all | solution.py:137
  85.5 0.0 copy-done
  85.5 1.5 %precondition.1 = (bf16[32,2,8,256]{3,2,1,0:T(8,128)(2,1)S(1)}, f32[2,2,256,256]{3,2,1,0:T(8,128)}) custom-call(f32[2,256]{1,0:T(2,128)S(1)} %get-tuple-element.8.used, bf16[32,2,8,256]{3,2,1,0:T(8,128)(2,1)S(1)} %all_to_all.21.rows, f32[2,2,256,256]{3,2,1,0:T(8,128)S(1)} %bitcast.5), custom_call_target="tpu_custom_call" | custom-call | tf_op jit(solution)/shard_map/precondition/pallas_call | solution.py:138
  87.1 44.1 %all_to_all.22.rows = bf16[32,2,8,256]{3,2,1,0:T(8,128)(2,1)S(1)} all-to-all(bf16[32,2,8,256]{3,2,1,0:T(8,128)(2,1)S(1)} %get-tuple-element.10), channel_id=1, replica_groups=mesh['fsdp'=32,'dp'=4,'mp'=8] {'fsdp'}, dimensions={0} | all-to-all | bytes 524288 | tf_op jit(solution)/shard_map/all_to_all | solution.py:146
  131.2 0.1 pick.1
  131.3 10.5 %all_to_all.23 = bf16[4,32,8,256]{3,2,1,0:T(8,128)(2,1)S(1)} all-to-all(bf16[4,32,8,256]{3,2,1,0:T(8,128)(2,1)S(1)} %pick.1), channel_id=1, replica_groups=mesh['fsdp'=32,'dp'=4,'mp'=8] {'dp'}, dimensions={0} | all-to-all | bytes 1048576 | tf_op jit(solution)/shard_map/all_to_all | solution.py:156
  141.8 0.8 copy.6
Async XLA Ops:
  0.6 84.9 %copy-start = (f32[1,1,2,2,256,256]{5,4,3,2,1,0:T(8,128)S(1)}, f32[1,1,2,2,256,256]{5,4,3,2,1,0:T(8,128)}, u32[]{:S(2)}) copy-start(f32[1,1,2,2,256,256]{5,4,3,2,1,0:T(8,128)} %param.5) | copy-start | bytes 3145732
